TPU v7x, 768 devices: a whole 4x8x12 slice. The times are simulated.
768 devices in a mesh: row: 48 (over z, x), col: 16 (over y, core).
Axes of the slice: x: 4, y: 8, z: 12, core: 2. Of those that a mesh axis runs over, the one named last changes fastest.
Arguments:
- amplitudes: bfloat16 [96, 128, 128, 128], P('row', 'col'), may hold values from -6 to 6
- amplitude_mask: int32 [96, 128], P('row', 'col'), may hold values 0 or 1
- integrals: bfloat16 [48, 128, 128, 128], P('row', 'col'), may hold values from -0.046875 to 0.046875
- integral_mask: int32 [48, 128], P('row', 'col'), may hold values from 0 to 1, as said below
- owners: int32 [48, 1], replicated, may hold values from 0 to 15; in each aligned block of 48 rows (0 to 47, 48 to 95, ...) at most 4 rows name the same one
Outputs:
- residual: bfloat16 [96, 64, 128, 128], P('row', 'col')
Inputs may be any that keep to these rules, and one draw needn't show every extreme that they name: `integral_mask`: among the 8 cd tiles that one device holds of its ab tile at most 4 are 1, and exactly 4 on some devices. `owners`: each col index owns at least one and at most 4 ab tiles; one owns exactly 4.
All inputs are finite; a program needn't handle non-finite values. No bound on the sum of `amplitude_mask` on one device may be relied on, other than what follows from the above.
Results may differ from a plain program's by a relative error of at most 0.022.
Values may be sent and summed in bfloat16 or wider, within the bound.
A program may use at most 64 MiB of HBM per device.

v0:
```python
import jax
import jax.numpy as jnp
from jax import lax
from jax.sharding import PartitionSpec as P


def per_device(amplitudes, amplitude_mask, integrals, integral_mask, owners):
    amp_kept = amplitudes * amplitude_mask[:, :, None, None].astype(jnp.bfloat16)
    total_ab = owners.shape[0]
    int_kept = integrals * integral_mask[:, :, None, None].astype(jnp.bfloat16)
    contrib = jnp.einsum(
        "icxy,kcwy->ikxw",
        amp_kept,
        lax.all_gather(int_kept, "row", axis=0, tiled=True),
        preferred_element_type=jnp.float32,
    )
    col_count = lax.axis_size("col")
    slots_each = 3 * total_ab // (2 * col_count)
    owner_list = owners[:, 0]
    positions = jnp.arange(total_ab, dtype=jnp.int32)
    earlier = (owner_list[None, :] == owner_list[:, None]) & (
        positions[None, :] < positions[:, None]
    )
    ranks = jnp.sum(earlier.astype(jnp.int32), axis=1)
    slot_list = owner_list * slots_each + ranks
    all_slots = jnp.arange(col_count * slots_each, dtype=jnp.int32)
    matches = (slot_list[:, None] == all_slots[None, :]).astype(jnp.int32)
    source = jnp.sum(matches * positions[:, None], axis=0)
    filled = jnp.sum(matches, axis=0).astype(jnp.float32)
    routed = jnp.take(contrib, source, axis=1) * filled[None, :, None, None]
    reduced = lax.psum_scatter(routed.astype(jnp.bfloat16), "col", scatter_dimension=1, tiled=True)
    return reduced


def solution(mesh):
    return jax.shard_map(
        per_device,
        mesh=mesh,
        in_specs=(
            P("row", "col", None, None),
            P("row", "col"),
            P("row", "col", None, None),
            P("row", "col"),
            P(),
        ),
        out_specs=P("row", "col", None, None),
        check_vma=False,
    )
```

profile of v0, /device:TPU:1, one launch (start us, length us, event | category | flops | bytes accessed | tf_op | source)
XLA Modules:
  0.0 266.5 jit_solution(14015376607979483199)
XLA Ops:
  6.5 0.0 all-gather.2.cloned.1.call-start
  6.5 0.7 convert_bitcast_fusion
  7.2 1.7 broadcast_multiply_fusion
  8.9 0.0 all-gather.2.cloned.1.call-update
  9.0 0.0 reduce-scatter.2.cloned.1.call-start
  9.0 0.7 convert_element_type.34
  9.7 0.9 convert_reduce_fusion.1
  10.6 0.7 fusion.11
  11.3 0.1 convert_reduce_fusion
  11.4 160.4 %all-gather.2.cloned.1.call-done = bf16[48,8,128,128]{3,2,1,0:T(8,128)(2,1)} async-done(((bf16[1,8,128,128]{3,2,1,0:T(8,128)(2,1)}), bf16[48,8,128,128]{3,2,1,0:T(8,128)(2,1)}) %all-gather.2.cloned.1.call-update) | async-done | bytes 12582928 | tf_op jit(solution)/shard_map/all_gather | solution.py:14
  171.8 8.4 %fusion.3 = f32[2,48,128,128]{2,3,0,1:T(8,128)} fusion(bf16[48,8,128,128]{3,2,1,0:T(8,128)(2,1)} %all-gather.2.cloned.1.call-done, bf16[2,8,128,128]{3,2,1,0:T(8,128)(2,1)} %param.5, bf16[2,8]{1,0:T(2,128)(2,1)S(1)} %convert_element_type.34), kind=kOutput, calls=%fused_computation.5 | convolution fusion | flops 3222274048 | bytes 19398688 | tf_op jit(solution)/shard_map/icxy,kcwy->ikxw/dot_general | solution.py:11
  180.2 7.1 %gather_fusion = f32[64,2,128,128]{2,3,1,0:T(8,128)} fusion(f32[2,48,128,128]{2,3,0,1:T(8,128)} %fusion.3, s32[1024]{0:T(1024)S(1)} %pad_clamp_fusion), kind=kCustom, calls=%fused_computation | custom fusion | bytes 16777472 | tf_op jit(solution)/shard_map/jit(_take)/gather | solution.py:30
  187.3 7.0 %fusion.2 = bf16[2,64,128,128]{2,3,0,1:T(8,128)(2,1)} fusion(f32[64,2,128,128]{2,3,1,0:T(8,128)} %gather_fusion, f32[64]{0:T(128)S(1)} %convert_element_type.36, pred[64]{0:T(512)(128)(4,1)S(1)} %compare_and_fusion), kind=kLoop, calls=%fused_computation.4 | loop fusion | flops 6291456 | bytes 12583232 | tf_op jit(solution)/shard_map/convert_element_type | solution.py:31
  194.3 0.0 reduce-scatter.2.cloned.1.call-update
  194.3 63.6 %reduce-scatter.2.cloned.1.call-done = bf16[2,4,128,128]{2,3,0,1:T(8,128)(2,1)} async-done(((bf16[2,64,128,128]{2,3,0,1:T(8,128)(2,1)}), bf16[2,4,128,128]{2,3,0,1:T(8,128)(2,1)}) %reduce-scatter.2.cloned.1.call-update) | async-done | bytes 262160 | tf_op jit(solution)/shard_map/reduce_scatter | solution.py:31
  257.9 1.8 copy.8
  (4 shorter events, 0.0 us)
Async XLA Ops:
  6.5 165.3 %all-gather.2.cloned.1.call-start = ((), (), s32[]{:S(2)}) async-start(), calls=%async_computation.1 | async-start | bytes 12845056 | tf_op jit(solution)/shard_map/all_gather | solution.py:14
  9.0 248.9 %reduce-scatter.2.cloned.1.call-start = ((), (), s32[]{:S(2)}) async-start(), calls=%async_computation.2 | async-start | bytes 4456448 | tf_op jit(solution)/shard_map/reduce_scatter | solution.py:31
Sparse Core Ops, SparseCore 0:
  10.9 160.8 all-gather.1
  194.4 63.4 reduce-scatter.1
where the time goes:
time: 267 us; the launch traced here: 266 us
  waiting for transfers between devices  224 us (84%)
  between operations  13.4 us (5%)
  other arithmetic  11.7 us (4%)
  local copies, waits for them, and re-layouts  8.88 us (3%)
  matrix products  8.4 us (3%)
    all_gather x1, waiting for transfers between devices, per_device(): lax.all_gather(int_kept, 'row', axis=0, tiled=True)  160 us
    reduce_scatter x1, waiting for transfers between devices, per_device(): lax.psum_scatter(routed.astype(jnp.bfloat16), 'col', scatter_dimension=1,...  63.6 us
    dot_general x1, matrix products, per_device(): jnp.einsum('icxy,kcwy->ikxw', amp_kept, lax.all_gather(int_kept, 'row', a...  8.4 us
    gather x1, local copies, waits for them, and re-layouts, per_device(): routed = jnp.take(contrib, source, axis=1) * filled[None, :, None, None]  7.09 us
    convert_element_type x1, other arithmetic, per_device(): routed.astype(jnp.bfloat16)  6.96 us
  transfers between devices with their start and end apart: 2, of which 2 were waited for; matrix products, arithmetic and copies ran while one was open for 1% of the time, Pallas kernels for 0%

commit v1 on v0

v1 whole, which is shorter than its diff:
```python
import functools

import jax
import jax.numpy as jnp
from jax import lax
from jax.experimental import pallas as pl
from jax.experimental.pallas import tpu as pltpu
from jax.sharding import PartitionSpec as P


B = 128
X = 4
C = 8
V = 4
META = 16
UNIT = V * B + META
HALF = 256
F32 = jnp.float32
BF16 = jnp.bfloat16
I32 = jnp.int32


def orbit_colour(left, right, eye, row, col):
    step = jnp.dot(right.astype(BF16), left.astype(BF16), preferred_element_type=F32)
    reach = jnp.minimum(step + eye, 1.0)
    for _ in range(5):
        half = reach.astype(BF16)
        reach = jnp.minimum(jnp.dot(half, half, preferred_element_type=F32), 1.0)
    label_r = jnp.min(jnp.where(reach > 0.5, row, 999.0), axis=0, keepdims=True)
    label_c = jnp.min(jnp.where(reach > 0.5, col, 999.0), axis=1, keepdims=True)
    other_r = jnp.sum(left * label_c, axis=0, keepdims=True)
    other_c = jnp.sum(left * label_r, axis=1, keepdims=True)
    return jnp.where(label_r > other_r, 1.0, 0.0), jnp.where(label_c > other_c, 1.0, 0.0)


def flip(value):
    return value + 1.0 - 2.0 * (value - 2.0 * jnp.floor(value * 0.5))


def colours_of(owners):
    n = owners.shape[0]
    row_i = lax.broadcasted_iota(I32, (n, n), 0)
    col_i = lax.broadcasted_iota(I32, (n, n), 1)
    row, col = row_i.astype(F32), col_i.astype(F32)
    one = lambda cond: jnp.where(cond, 1.0, 0.0)
    eye = one(row_i == col_i)
    before_r, before_c = one(row_i < col_i), one(col_i < row_i)
    own_c = jnp.broadcast_to(owners, (n, n))
    own_r = jnp.sum(own_c * eye, axis=0, keepdims=True)
    same = one(own_c == own_r)
    over0 = lambda v: jnp.sum(v, axis=0, keepdims=True)
    over1 = lambda v: jnp.sum(v, axis=1, keepdims=True)
    rank_r, rank_c = over0(same * before_r), over1(same * before_c)
    count_r, count_c = over0(same), over1(same)
    even_r, even_c = one(flip(rank_r) > rank_r), one(flip(rank_c) > rank_c)
    lone_r, lone_c = even_r * one(rank_r == count_r - 1.0), even_c * one(rank_c == count_c - 1.0)
    nth_r, nth_c = over0(lone_c * before_r), over1(lone_r * before_c)
    left = one(row_i == (col_i ^ 1))
    right = same * one(rank_c == flip(rank_r)) + lone_c * lone_r * one(nth_c == flip(nth_r))
    first_r, first_c = orbit_colour(left, right, eye, row, col)
    alike = one(first_c == first_r)
    apart = 1.0 - eye
    left = one((row_i // X) == (col_i // X)) * alike * apart
    right = same * alike * apart
    lone_r, lone_c = 1.0 - over0(right), 1.0 - over1(right)
    nth_r, nth_c = over0(lone_c * alike * before_r), over1(lone_r * alike * before_c)
    right = right + lone_c * lone_r * alike * one(nth_c == flip(nth_r))
    second_r, _ = orbit_colour(left, right, eye, row, col)
    return 2.0 * first_r + second_r, rank_r, own_r


TABLE = 40


def table_of(owners, me_x, me_z, me_col, cols):
    colour, rank, own = colours_of(owners.astype(F32))
    n = owners.shape[0]

    def part(rows, make):
        at = lax.broadcasted_iota(I32, (rows, n), 0).astype(F32)
        edge = lax.broadcasted_iota(I32, (rows, n), 1)
        return jnp.sum(make(at, (edge // X).astype(F32), (edge % X).astype(F32)), axis=1, keepdims=True)

    x, z, d = me_x.astype(F32), me_z.astype(F32), me_col.astype(F32)
    slots = part(cols, lambda at, ez, ex: jnp.where((own == at) & (colour == x), ez + 1.0, 0.0))
    mine = part(8, lambda at, ez, ex: jnp.where((rank == at) & (own == d), colour + 1.0, 0.0))
    unit = part(8, lambda at, ez, ex: jnp.where((colour == x) & (ez == z), ex, 0.0))
    spare = jnp.zeros((TABLE - cols - 16, 1), F32)
    rows = jnp.concatenate([slots, mine, unit, spare], axis=0)
    return jnp.broadcast_to(rows, (TABLE, 128)).astype(I32)


def kernel(
    Z, Y, amp, amp_mask, integral, int_mask, owners, out,
    A, XI, G, mine, part_out, part_in, ring_out, ring_in, met, table_v, table_s, meta_v, meta_s,
    xi_send, xi_recv, a_send, a_recv, z_send, z_recv, p_send, p_recv, r_send, r_recv, m_send, m_recv, local,
):
    row, col = lax.axis_index("row"), lax.axis_index("col")
    x, z, y, core = row % X, row // X, col // 2, col % 2

    def at_x(shift):
        return (z * X + (x + shift) % X, col)

    def at_z(shift):
        return (((z + shift) % Z) * X + x, col)

    def at_y(shift):
        return (row, ((y + shift) % Y) * 2 + core)

    partner = (row, y * 2 + (1 - core))

    barrier = pltpu.get_barrier_semaphore()
    peers = [at_x(1), at_x(2), at_x(3), at_z(1), at_z(Z - 1), at_y(1), at_y(Y - 1), partner]
    for peer in peers:
        pl.semaphore_signal(barrier, inc=1, device_id=peer, device_id_type=pl.DeviceIdType.MESH)

    def copy(src, dst, send, recv, to):
        return pltpu.make_async_remote_copy(
            src_ref=src, dst_ref=dst, send_sem=send, recv_sem=recv, device_id=to,
            device_id_type=pl.DeviceIdType.MESH,
        )

    kept = [int_mask[0, c] for c in range(C)]
    before, places = jnp.int32(0), [jnp.int32(0)] * V
    for c in range(C):
        for j in range(V):
            places[j] = jnp.where((kept[c] != 0) & (before == j), c, places[j])
        before = before + kept[c]
    for j in range(V):
        scale = jnp.where(before > j, 1.0, 0.0).astype(BF16)
        XI[0, j * B:(j + 1) * B, :] = integral[0, places[j]] * scale
    at = lax.broadcasted_iota(I32, (META, B), 0)
    meta = jnp.zeros((META, B), I32)
    for j in range(V):
        meta = jnp.where(at == j, places[j], meta)
    XI[0, V * B:UNIT, :] = meta.astype(F32).astype(BF16)

    pl.semaphore_wait(barrier, len(peers))

    xi_right = copy(XI.at[0], XI.at[3], xi_send.at[0], xi_recv.at[0], at_x(1))
    xi_left = copy(XI.at[0], XI.at[1], xi_send.at[1], xi_recv.at[1], at_x(3))
    xi_right.start()
    xi_left.start()

    for i in range(2):
        for c in range(C):
            A[i, c] = amp[i, c] * amp_mask[i, c].astype(F32).astype(BF16)

    a_copies = [
        copy(A.at[0], A.at[6], a_send.at[0], a_recv.at[0], at_x(1)),
        copy(A.at[1], A.at[3], a_send.at[1], a_recv.at[1], at_x(3)),
        copy(A.at[1], A.at[7], a_send.at[2], a_recv.at[2], at_x(1)),
        copy(A.at[0], A.at[2], a_send.at[3], a_recv.at[3], at_x(3)),
    ]
    a_on_right = copy(A.at[6], A.at[4], a_send.at[4], a_recv.at[4], at_x(1))
    a_on_left = copy(A.at[3], A.at[5], a_send.at[5], a_recv.at[5], at_x(3))

    table_v[...] = table_of(owners[...], x, z, col, 2 * Y)
    table_copy = pltpu.make_async_copy(table_v, table_s, local.at[0])
    table_copy.start()

    xi_on_right = copy(XI.at[3, 0:HALF], XI.at[2, 0:HALF], xi_send.at[2], xi_recv.at[2], at_x(1))
    xi_on_left = copy(XI.at[1, HALF:UNIT], XI.at[2, HALF:UNIT], xi_send.at[3], xi_recv.at[3], at_x(3))
    xi_right.wait_recv()
    xi_on_right.start()
    xi_left.wait_recv()
    xi_on_left.start()
    for c in a_copies:
        c.start()
    table_copy.wait()
    xi_on_right.wait_recv()
    xi_on_left.wait_recv()

    G[0] = XI[(jnp.clip(table_s[2 * Y + 8, 0], 0, X - 1) - x + X) % X]

    def meta_out(rel):
        meta_v[rel] = G[rel, V * B:UNIT, :].astype(F32).astype(I32)[0:8]
        pltpu.make_async_copy(meta_v.at[rel], meta_s.at[rel], local.at[1 + rel]).start()

    steps = Z // 2 - 1
    to_right, to_left = [], []
    for s in range(steps):
        to_right.append(copy(G.at[(Z - s) % Z], G.at[Z - 1 - s], z_send.at[0, s], z_recv.at[0, s], at_z(1)))
        to_left.append(copy(G.at[s], G.at[s + 1], z_send.at[1, s], z_recv.at[1, s], at_z(Z - 1)))
    far = Z // 2
    to_right.append(copy(
        G.at[far + 1, 0:HALF], G.at[far, 0:HALF], z_send.at[0, steps], z_recv.at[0, steps], at_z(1)))
    to_left.append(copy(
        G.at[far - 1, HALF:UNIT], G.at[far, HALF:UNIT], z_send.at[1, steps], z_recv.at[1, steps], at_z(Z - 1)))

    to_right[0].start()
    to_left[0].start()
    meta_out(0)
    for s in range(steps):
        to_right[s].wait_recv()
        to_right[s + 1].start()
        to_left[s].wait_recv()
        to_left[s + 1].start()
        meta_out(Z - 1 - s)
        meta_out(s + 1)
        if s == 2:
            a_copies[0].wait_recv()
            a_on_right.start()
            a_copies[1].wait_recv()
            a_on_left.start()
    to_right[steps].wait_recv()
    to_left[steps].wait_recv()
    meta_out(far)
    a_copies[2].wait_recv()
    a_copies[3].wait_recv()
    a_on_right.wait_recv()
    a_on_left.wait_recv()
    for rel in range(Z):
        pltpu.make_async_copy(meta_v.at[rel], meta_s.at[rel], local.at[1 + rel]).wait()

    FLOW = ((0, 1), (3, 2))

    def part_copy(s):
        return copy(part_out.at[s], part_in.at[s], p_send.at[s], p_recv.at[s], partner)

    def ring_copy(s, way, sub):
        return copy(
            ring_out.at[s, way, sub], ring_in.at[s + 1, way, sub], r_send.at[s, way, sub], r_recv.at[s, way, sub],
            at_y(1 if way == 0 else Y - 1),
        )

    def products(s):
        for way in range(2):
            slot_y = (y - 1 - s + 2 * Y) % Y if way == 0 else (y + 1 + s) % Y
            for whose in (1, 0):
                owner = slot_y * 2 + (core if whose == 0 else 1 - core)
                named = table_s[owner, 0]
                filled = jnp.where(named > 0, 1.0, 0.0).astype(F32)
                rel = jnp.clip(named - 1, 0, Z - 1) - z
                rel = jnp.where(rel < 0, rel + Z, rel)
                where = [jnp.clip(meta_s[rel, j, 0], 0, C - 1) for j in range(V)]
                unit = G[rel, 0:V * B, :]
                pairs = [
                    jnp.concatenate([unit[j * B:(j + 1) * B], unit[(j + 1) * B:(j + 2) * B]], axis=1)
                    for j in range(0, V, 2)
                ]
                for sub in range(2):
                    r = FLOW[way][sub]
                    total = None
                    for p, pair in enumerate(pairs):
                        tiles = jnp.concatenate(
                            [A[2 * r:2 * r + 2, where[2 * p + q]].reshape(2 * B, B) for q in range(2)], axis=1)
                        term = lax.dot_general(tiles, pair, (((1,), (1,)), ((), ())), preferred_element_type=F32)
                        total = term if total is None else total + term
                    total = total * filled
                    if whose == 0:
                        mine[s, way, sub] = total
                    else:
                        part_out[s, way, sub] = total.astype(BF16)
        part_copy(s).start()

    ring_in[0] = jnp.zeros_like(ring_in[0])
    products(0)

    def ring_step(s, carry):
        part_copy(s).wait_recv()
        for sub in range(2):
            for way in range(2):
                @pl.when(s > 0)
                def _():
                    ring_copy(s - 1, way, sub).wait_recv()
                total = mine[s, way, sub] + part_in[s, way, sub].astype(F32) + ring_in[s, way, sub].astype(F32)
                ring_out[s, way, sub] = total.astype(BF16)
                ring_copy(s, way, sub).start()
        products(s + 1)
        return carry

    lax.fori_loop(0, Y - 1, ring_step, jnp.int32(0))

    def met_copy(r):
        return copy(ring_out.at[Y - 1, *PLACE[r]], met.at[X - r], m_send.at[r - 1], m_recv.at[r - 1], at_x(r))

    PLACE = {FLOW[way][sub]: (way, sub) for way in range(2) for sub in range(2)}
    last = Y - 1
    part_copy(last).wait_recv()
    for sub in range(2):
        for way in range(2):
            r = FLOW[way][sub]
            ring_copy(last - 1, way, sub).wait_recv()
            total = mine[last, way, sub] + part_in[last, way, sub].astype(F32) + ring_in[last, way, sub].astype(F32)
            if r == 0:
                met[0] = total.astype(BF16)
            else:
                ring_out[last, way, sub] = total.astype(BF16)
                met_copy(r).start()
    for r in range(1, X):
        met_copy(r).wait_recv()
    slots = out.shape[1]
    for t in range(slots):
        named = table_s[2 * Y + t, 0]
        filled = jnp.where(named > 0, 1.0, 0.0).astype(BF16)
        rel = jnp.clip(named - 1, 0, X - 1) - x
        tiles = met[jnp.where(rel < 0, rel + X, rel)] * filled
        for i in range(2):
            out[i, t] = tiles[i * B:(i + 1) * B]

    for c in [xi_right, xi_left, xi_on_right, xi_on_left, *a_copies, a_on_right, a_on_left, *to_right, *to_left]:
        c.wait_send()

    def sent(s, carry):
        part_copy(s).wait_send()
        for sub in range(2):
            for way in range(2):
                ring_copy(s, way, sub).wait_send()
        return carry

    lax.fori_loop(0, Y - 1, sent, jnp.int32(0))
    part_copy(last).wait_send()
    for r in range(1, X):
        met_copy(r).wait_send()


def per_device(Z, Y, amplitudes, amplitude_mask, integrals, integral_mask, owners):
    vmem = pl.BlockSpec(memory_space=pltpu.VMEM)
    smem = pl.BlockSpec(memory_space=pltpu.SMEM)
    dma = pltpu.SemaphoreType.DMA
    steps = Z // 2
    pair = 2 * B
    return pl.pallas_call(
        functools.partial(kernel, Z, Y),
        out_shape=jax.ShapeDtypeStruct((2, 4, B, B), BF16),
        in_specs=[vmem, smem, vmem, smem, vmem],
        out_specs=vmem,
        scratch_shapes=[
            pltpu.VMEM((2 * X, C, B, B), BF16),
            pltpu.VMEM((X, UNIT, B), BF16),
            pltpu.VMEM((Z, UNIT, B), BF16),
            pltpu.VMEM((Y, 2, 2, pair, B), F32),
            pltpu.VMEM((Y, 2, 2, pair, B), BF16),
            pltpu.VMEM((Y, 2, 2, pair, B), BF16),
            pltpu.VMEM((Y, 2, 2, pair, B), BF16),
            pltpu.VMEM((Y, 2, 2, pair, B), BF16),
            pltpu.VMEM((X, pair, B), BF16),
            pltpu.VMEM((TABLE, 128), I32),
            pltpu.SMEM((TABLE, 128), I32),
            pltpu.VMEM((Z, 8, 128), I32),
            pltpu.SMEM((Z, 8, 128), I32),
            dma((4,)), dma((4,)),
            dma((6,)), dma((6,)),
            dma((2, steps)), dma((2, steps)),
            dma((Y,)), dma((Y,)),
            dma((Y - 1, 2, 2)), dma((Y - 1, 2, 2)),
            dma((X - 1,)), dma((X - 1,)),
            dma((1 + Z,)),
        ],
        compiler_params=pltpu.CompilerParams(
            collective_id=0, has_side_effects=True, vmem_limit_bytes=48 * 1024 * 1024),
        cost_estimate=pl.CostEstimate(flops=2 * 128 * 4 * B * B * B, bytes_accessed=1 << 20, transcendentals=0),
    )(amplitudes, amplitude_mask, integrals, integral_mask, owners)


def solution(mesh):
    Z, Y = mesh.shape["row"] // X, mesh.shape["col"] // 2
    return jax.shard_map(
        functools.partial(per_device, Z, Y),
        mesh=mesh,
        in_specs=(
            P("row", "col", None, None),
            P("row", "col"),
            P("row", "col", None, None),
            P("row", "col"),
            P(),
        ),
        out_specs=P("row", "col", None, None),
        check_vma=False,
    )
```

time: 267 us -> 94 us (0.35)
  waiting for transfers between devices: 224 us -> 0 us
  Pallas kernels: 0 us -> 90.3 us
  between operations: 13.4 us -> 0.02 us
  other arithmetic: 11.7 us -> 0 us
  matrix products: 8.4 us -> 0 us
  local copies, waits for them, and re-layouts: 8.88 us -> 3.47 us
    all_gather x1 -> x0, waiting for transfers between devices: 160 us -> none  [per_device(): lax.all_gather(int_kept, 'row', axis=0, tiled=True)]
    pallas_call x0 -> x1, Pallas kernels: none -> 90.3 us  [per_device(): pl.pallas_call(functools.partial(kernel, Z, Y), out_shape=jax.ShapeDtypeS...]
    reduce_scatter x1 -> x0, waiting for transfers between devices: 63.6 us -> none  [per_device(): lax.psum_scatter(routed.astype(jnp.bfloat16), 'col', scatter_dimension=1,...]
    dot_general x1 -> x0, matrix products: 8.4 us -> none  [per_device(): jnp.einsum('icxy,kcwy->ikxw', amp_kept, lax.all_gather(int_kept, 'row', a...]
    convert_element_type x4 -> x0, other arithmetic: 8.31 us -> none  [the longest x1 6.96 us: per_device(): routed.astype(jnp.bfloat16)]
    gather x1 -> x0, local copies, waits for them, and re-layouts: 7.09 us -> none  [per_device(): routed = jnp.take(contrib, source, axis=1) * filled[None, :, None, None]]
    unnamed x0 -> x10, local copies, waits for them, and re-layouts: none -> 3.47 us
  transfers between devices with their start and end apart: 2 -> 0, of which waited for: 2 -> 0; matrix products, arithmetic and copies ran while one was open for 1% -> 0% of each run, Pallas kernels for 0% -> 0%
where the time goes in v1:
time: 94 us; the launch traced here: 93.8 us
  Pallas kernels  90.3 us (96%)
  local copies, waits for them, and re-layouts  3.47 us (4%)
    pallas_call x1, Pallas kernels, per_device(): pl.pallas_call(functools.partial(kernel, Z, Y), out_shape=jax.ShapeDtypeS...  90.3 us
    unnamed x10, local copies, waits for them, and re-layouts  3.47 us

profile of v1, /device:TPU:1, one launch (start us, length us, event | category | flops | bytes accessed | tf_op | source)
XLA Modules:
  0.0 93.8 jit_solution(3511984474726777199)
XLA Ops:
  0.0 0.0 copy-start.3
  0.0 0.0 copy-start.2
  0.0 0.8 copy.6.owners
  0.8 0.0 copy-done.3
  0.8 0.0 copy-done.2
  0.8 0.0 copy-start
  0.8 1.0 %copy-done = bf16[2,8,128,128]{3,2,1,0:T(8,128)(2,1)S(1)} copy-done((bf16[2,8,128,128]{3,2,1,0:T(8,128)(2,1)S(1)}, bf16[2,8,128,128]{3,2,1,0:T(8,128)(2,1)}, u32[]{:S(2)}) %copy-start) | copy-done | bytes 524312
  1.8 0.0 copy-start.1
  1.8 0.9 %copy-done.1 = bf16[1,8,128,128]{3,2,1,0:T(8,128)(2,1)S(1)} copy-done((bf16[1,8,128,128]{3,2,1,0:T(8,128)(2,1)S(1)}, bf16[1,8,128,128]{3,2,1,0:T(8,128)(2,1)}, u32[]{:S(2)}) %copy-start.1) | copy-done | bytes 262168
  2.8 90.3 %shard_map.55 = bf16[2,4,128,128]{3,2,1,0:T(8,128)(2,1)S(1)} custom-call(bf16[2,8,128,128]{3,2,1,0:T(8,128)(2,1)S(1)} %copy-done, s32[2,8]{1,0:T(2,128)S(1)} %copy-done.2, bf16[1,8,128,128]{3,2,1,0:T(8,128)(2,1)S(1)} %copy-done.1, s32[1,8]{1,0:T(1,128)S(1)} %copy-done.3, s32[48,1]{1,0:T(8,128)S(1)} %copy.6.owners), custom_call_target="tpu_custom_call" | custom-call | flops 2147483648 | bytes 1048576 | tf_op jit(solution)/shard_map/pallas_call | solution.py:324
  93.1 0.7 copy.8
Async XLA Ops:
  0.0 0.8 copy-start.3
  0.0 0.8 copy-start.2
  0.8 1.0 %copy-start = (bf16[2,8,128,128]{3,2,1,0:T(8,128)(2,1)S(1)}, bf16[2,8,128,128]{3,2,1,0:T(8,128)(2,1)}, u32[]{:S(2)}) copy-start(bf16[2,8,128,128]{3,2,1,0:T(8,128)(2,1)} %amp.1) | copy-start | bytes 1572868
  1.8 0.9 %copy-start.1 = (bf16[1,8,128,128]{3,2,1,0:T(8,128)(2,1)S(1)}, bf16[1,8,128,128]{3,2,1,0:T(8,128)(2,1)}, u32[]{:S(2)}) copy-start(bf16[1,8,128,128]{3,2,1,0:T(8,128)(2,1)} %integral.1) | copy-start | bytes 786436

commit v2 on v1

v2 whole, which is shorter than its diff:
```python
import functools

import jax
import jax.numpy as jnp
from jax import lax
from jax.experimental import pallas as pl
from jax.experimental.pallas import tpu as pltpu
from jax.sharding import PartitionSpec as P


B = 128
X = 4
C = 8
V = 4
META = 16
UNIT = V * B + META
HALF = 256
F32 = jnp.float32
BF16 = jnp.bfloat16
I32 = jnp.int32


def orbit_colour(left, right, eye, row, col):
    step = jnp.dot(right.astype(BF16), left.astype(BF16), preferred_element_type=F32)
    reach = jnp.minimum(step + eye, 1.0)
    for _ in range(5):
        half = reach.astype(BF16)
        reach = jnp.minimum(jnp.dot(half, half, preferred_element_type=F32), 1.0)
    label_r = jnp.min(jnp.where(reach > 0.5, row, 999.0), axis=0, keepdims=True)
    label_c = jnp.min(jnp.where(reach > 0.5, col, 999.0), axis=1, keepdims=True)
    other_r = jnp.sum(left * label_c, axis=0, keepdims=True)
    other_c = jnp.sum(left * label_r, axis=1, keepdims=True)
    return jnp.where(label_r > other_r, 1.0, 0.0), jnp.where(label_c > other_c, 1.0, 0.0)


def flip(value):
    return value + 1.0 - 2.0 * (value - 2.0 * jnp.floor(value * 0.5))


def colours_of(owners):
    n = owners.shape[1]
    row_i = lax.broadcasted_iota(I32, (n, n), 0)
    col_i = lax.broadcasted_iota(I32, (n, n), 1)
    row, col = row_i.astype(F32), col_i.astype(F32)
    one = lambda cond: jnp.where(cond, 1.0, 0.0)
    eye = one(row_i == col_i)
    before_r, before_c = one(row_i < col_i), one(col_i < row_i)
    own_r = jnp.broadcast_to(owners, (n, n))
    own_c = jnp.sum(own_r * eye, axis=1, keepdims=True)
    same = one(own_c == own_r)
    over0 = lambda v: jnp.sum(v, axis=0, keepdims=True)
    over1 = lambda v: jnp.sum(v, axis=1, keepdims=True)
    rank_r, rank_c = over0(same * before_r), over1(same * before_c)
    count_r, count_c = over0(same), over1(same)
    even_r, even_c = one(flip(rank_r) > rank_r), one(flip(rank_c) > rank_c)
    lone_r, lone_c = even_r * one(rank_r == count_r - 1.0), even_c * one(rank_c == count_c - 1.0)
    nth_r, nth_c = over0(lone_c * before_r), over1(lone_r * before_c)
    left = one(row_i == (col_i ^ 1))
    right = same * one(rank_c == flip(rank_r)) + lone_c * lone_r * one(nth_c == flip(nth_r))
    first_r, first_c = orbit_colour(left, right, eye, row, col)
    alike = one(first_c == first_r)
    apart = 1.0 - eye
    left = one((row_i // X) == (col_i // X)) * alike * apart
    right = same * alike * apart
    lone_r, lone_c = 1.0 - over0(right), 1.0 - over1(right)
    nth_r, nth_c = over0(lone_c * alike * before_r), over1(lone_r * alike * before_c)
    right = right + lone_c * lone_r * alike * one(nth_c == flip(nth_r))
    second_r, _ = orbit_colour(left, right, eye, row, col)
    return 2.0 * first_r + second_r, rank_r


TABLE = 40


def table_of(owners, me_x, me_z, me_col, cols):
    own = owners.astype(F32)
    colour, rank = colours_of(own)
    n = owners.shape[1]

    def part(rows, make):
        at = lax.broadcasted_iota(I32, (rows, n), 0).astype(F32)
        edge = lax.broadcasted_iota(I32, (rows, n), 1)
        return jnp.sum(make(at, (edge // X).astype(F32), (edge % X).astype(F32)), axis=1, keepdims=True)

    x, z, d = me_x.astype(F32), me_z.astype(F32), me_col.astype(F32)
    slots = part(cols, lambda at, ez, ex: jnp.where((own == at) & (colour == x), ez + 1.0, 0.0))
    mine = part(8, lambda at, ez, ex: jnp.where((rank == at) & (own == d), colour + 1.0, 0.0))
    unit = part(8, lambda at, ez, ex: jnp.where((colour == x) & (ez == z), ex, 0.0))
    spare = jnp.zeros((TABLE - cols - 16, 1), F32)
    rows = jnp.concatenate([slots, mine, unit, spare], axis=0)
    return jnp.broadcast_to(rows, (TABLE, 128)).astype(I32)


LATE = ((2, 0), (1, 3))
ORDER = [(way, LATE[1 - way][k] if early else LATE[way][k])
         for early in (True, False) for k in range(2) for way in range(2)]


def kernel(
    Z, Y, amp_hbm, amp_mask, int_hbm, int_mask, owners, out,
    amp, integral, A, XI0, XI1, G, mine, part_out, part_in, ring_out, ring_in, met, table_v, table_s, meta_v, meta_s,
    xi_send, xi_recv, a_send, a_recv, z_send, z_recv, p_send, p_recv, r_send, r_recv, m_send, m_recv, local,
):
    row, col = lax.axis_index("row"), lax.axis_index("col")
    x, z, y, core = row % X, row // X, col // 2, col % 2

    int_in = pltpu.make_async_copy(int_hbm, integral, local.at[Z + 1])
    amp_in = pltpu.make_async_copy(amp_hbm, amp, local.at[Z + 2])
    int_in.start()
    amp_in.start()

    def at_x(shift):
        return (z * X + (x + shift) % X, col)

    def at_z(shift):
        return (((z + shift) % Z) * X + x, col)

    def at_y(shift):
        return (row, ((y + shift) % Y) * 2 + core)

    partner = (row, y * 2 + (1 - core))

    barrier = pltpu.get_barrier_semaphore()
    peers = [at_x(1), at_x(2), at_x(3), at_z(1), at_z(Z - 1), at_y(1), at_y(Y - 1), partner]
    for peer in peers:
        pl.semaphore_signal(barrier, inc=1, device_id=peer, device_id_type=pl.DeviceIdType.MESH)

    def copy(src, dst, send, recv, to):
        return pltpu.make_async_remote_copy(
            src_ref=src, dst_ref=dst, send_sem=send, recv_sem=recv, device_id=to,
            device_id_type=pl.DeviceIdType.MESH,
        )

    int_in.wait()
    kept = [int_mask[0, c] for c in range(C)]
    before, places = jnp.int32(0), [jnp.int32(0)] * V
    for c in range(C):
        for j in range(V):
            places[j] = jnp.where((kept[c] != 0) & (before == j), c, places[j])
        before = before + kept[c]
    XI = (XI0, XI1)
    for j in range(V):
        scale = jnp.where(before > j, 1.0, 0.0).astype(BF16)
        XI[j // 2][0, (j % 2) * B:(j % 2 + 1) * B, :] = integral[0, places[j]] * scale
    at = lax.broadcasted_iota(I32, (META, B), 0)
    meta = jnp.zeros((META, B), I32)
    for j in range(V):
        meta = jnp.where(at == j, places[j], meta)
    XI1[0, V * B - HALF:UNIT - HALF, :] = meta.astype(F32).astype(BF16)

    pl.semaphore_wait(barrier, len(peers))

    PARTS = (pl.ds(0, HALF), pl.ds(HALF, UNIT - HALF))
    xi_copies = [
        [copy(XI[h].at[0], XI[h].at[X - r], xi_send.at[h, r - 1], xi_recv.at[h, r - 1], at_x(r)) for r in (2, 1, 3)]
        for h in range(2)
    ]
    for h in range(2):
        for c in xi_copies[h]:
            c.start()

    amp_in.wait()
    for i in range(2):
        for c in range(C):
            A[i, c] = amp[i, c] * amp_mask[i, c].astype(F32).astype(BF16)
    for way in range(2):
        for r in LATE[1 - way]:
            ring_in[way, 0, r] = jnp.zeros_like(ring_in[way, 0, r])

    a_copies = [
        copy(A.at[0], A.at[6], a_send.at[0], a_recv.at[0], at_x(1)),
        copy(A.at[1], A.at[3], a_send.at[1], a_recv.at[1], at_x(3)),
        copy(A.at[1], A.at[7], a_send.at[2], a_recv.at[2], at_x(1)),
        copy(A.at[0], A.at[2], a_send.at[3], a_recv.at[3], at_x(3)),
    ]
    a_on_right = copy(A.at[6], A.at[4], a_send.at[4], a_recv.at[4], at_x(1))
    a_on_left = copy(A.at[3], A.at[5], a_send.at[5], a_recv.at[5], at_x(3))

    table_v[...] = table_of(owners[...], x, z, col, 2 * Y)
    table_copy = pltpu.make_async_copy(table_v, table_s, local.at[0])
    table_copy.start()

    far = Z // 2
    to_right = [
        [copy(G.at[(Z - s) % Z, rows], G.at[Z - 1 - s, rows], z_send.at[0, s, h], z_recv.at[0, s, h], at_z(1))
         for h, rows in enumerate(PARTS) if s < far - 1 or h == 0]
        for s in range(far)
    ]
    to_left = [
        [copy(G.at[s, rows], G.at[s + 1, rows], z_send.at[1, s, h], z_recv.at[1, s, h], at_z(Z - 1))
         for h, rows in enumerate(PARTS) if s < far - 1 or h == 1]
        for s in range(far)
    ]

    table_copy.wait()
    from_rel = (jnp.clip(table_s[2 * Y + 8, 0], 0, X - 1) - x + X) % X
    for h, rows in enumerate(PARTS):
        for c in xi_copies[h]:
            c.wait_recv()
        G[0, rows] = XI[h][from_rel]
        to_right[0][h].start()
        to_left[0][h].start()
    for c in a_copies:
        c.start()

    def meta_out(rel):
        meta_v[rel] = G[rel, V * B:UNIT, :].astype(F32).astype(I32)[0:8]
        pltpu.make_async_copy(meta_v.at[rel], meta_s.at[rel], local.at[1 + rel]).start()

    meta_out(0)
    for s in range(far - 1):
        for h in range(2):
            to_right[s][h].wait_recv()
            if s + 1 < far - 1 or h == 0:
                to_right[s + 1][h].start()
            to_left[s][h].wait_recv()
            if s + 1 < far - 1:
                to_left[s + 1][h].start()
            elif h == 1:
                to_left[s + 1][0].start()
        meta_out(Z - 1 - s)
        meta_out(s + 1)
        if s == 2:
            a_copies[0].wait_recv()
            a_on_right.start()
            a_copies[1].wait_recv()
            a_on_left.start()
    to_right[far - 1][0].wait_recv()
    to_left[far - 1][0].wait_recv()
    meta_out(far)
    a_copies[2].wait_recv()
    a_copies[3].wait_recv()
    a_on_right.wait_recv()
    a_on_left.wait_recv()
    for rel in range(Z):
        pltpu.make_async_copy(meta_v.at[rel], meta_s.at[rel], local.at[1 + rel]).wait()

    far_y = Y // 2

    def part_copy(n):
        return copy(part_out.at[n], part_in.at[n], p_send.at[n], p_recv.at[n], partner)

    def ring_copy(s, way, r):
        return copy(
            ring_out.at[way, s, r], ring_in.at[way, s, r], r_send.at[way, s, r], r_recv.at[way, s, r],
            at_y(1 if way == 0 else Y - 1),
        )

    def products(n, slot_y):
        for whose in (1, 0):
            owner = slot_y * 2 + (core + whose) % 2
            named = table_s[owner, 0]
            filled = jnp.where(named > 0, 1.0, 0.0).astype(F32)
            rel = jnp.clip(named - 1, 0, Z - 1) - z
            rel = jnp.where(rel < 0, rel + Z, rel)
            where = [jnp.clip(meta_s[rel, j, 0], 0, C - 1) for j in range(V)]
            unit = G[rel, 0:V * B, :]
            wide = jnp.concatenate([unit[j * B:(j + 1) * B] for j in range(V)], axis=1)
            for r in range(X):
                tiles = jnp.concatenate([A[2 * r:2 * r + 2, where[j]].reshape(2 * B, B) for j in range(V)], axis=1)
                total = filled * lax.dot_general(tiles, wide, (((1,), (1,)), ((), ())), preferred_element_type=F32)
                if whose == 0:
                    mine[n, r] = total
                else:
                    part_out[n, r] = total.astype(BF16)
            if whose == 1:
                part_copy(n).start()

    def one(way, s):
        products(2 * s + way, (y + (far_y - s if way == 0 else far_y + s)) % Y)

    products(0, (y + far_y) % Y)
    one(0, 1)
    part_copy(0).wait_recv()
    for k in range(2):
        for way in range(2):
            r = LATE[way][k]
            ring_out[way, 0, r] = (mine[0, r] + part_in[0, r].astype(F32)).astype(BF16)
            ring_copy(0, way, r).start()
    one(1, 1)

    def ring_step(s, carry):
        part_copy(2 * s).wait_recv()
        part_copy(2 * s + 1).wait_recv()
        for way, r in ORDER:
            if r in LATE[way]:
                ring_copy(s - 1, way, r).wait_recv()
            else:
                @pl.when(s > 1)
                def _():
                    ring_copy(s - 1, way, r).wait_recv()
            n = 2 * s + way
            total = mine[n, r] + part_in[n, r].astype(F32) + ring_in[way, s - 1, r].astype(F32)
            ring_out[way, s, r] = total.astype(BF16)
            ring_copy(s, way, r).start()

        @pl.when(s < far_y - 1)
        def _():
            one(0, s + 1)
            one(1, s + 1)
        return carry

    lax.fori_loop(1, far_y, ring_step, jnp.int32(0))
    products(1, y)

    def met_copy(r):
        return copy(ring_out.at[0, far_y, r], met.at[X - r], m_send.at[r - 1], m_recv.at[r - 1], at_x(r))

    last = far_y - 1
    part_copy(1).wait_recv()
    for way, r in ORDER:
        ring_copy(last, way, r).wait_recv()
        if r in LATE[way]:
            total = (mine[1, r] + part_in[1, r].astype(F32)) + (
                ring_in[0, last, r].astype(F32) + ring_in[1, last, r].astype(F32))
            if r == 0:
                met[0] = total.astype(BF16)
            else:
                ring_out[0, far_y, r] = total.astype(BF16)
                met_copy(r).start()
    for r in range(1, X):
        met_copy(r).wait_recv()
    slots = out.shape[1]
    for t in range(slots):
        named = table_s[2 * Y + t, 0]
        filled = jnp.where(named > 0, 1.0, 0.0).astype(BF16)
        rel = jnp.clip(named - 1, 0, X - 1) - x
        tiles = met[jnp.where(rel < 0, rel + X, rel)] * filled
        for i in range(2):
            out[i, t] = tiles[i * B:(i + 1) * B]

    for c in [*xi_copies[0], *xi_copies[1], *a_copies, a_on_right, a_on_left]:
        c.wait_send()
    for s in range(far):
        for c in to_right[s] + to_left[s]:
            c.wait_send()
    for n in range(Y):
        part_copy(n).wait_send()
    for s in range(far_y):
        for way, r in ORDER:
            if s > 0 or r in LATE[way]:
                ring_copy(s, way, r).wait_send()
    for r in range(1, X):
        met_copy(r).wait_send()


def per_device(Z, Y, amplitudes, amplitude_mask, integrals, integral_mask, owners):
    vmem = pl.BlockSpec(memory_space=pltpu.VMEM)
    smem = pl.BlockSpec(memory_space=pltpu.SMEM)
    hbm = pl.BlockSpec(memory_space=pl.ANY)
    dma = pltpu.SemaphoreType.DMA
    far, far_y = Z // 2, Y // 2
    piece = 2 * B
    return pl.pallas_call(
        functools.partial(kernel, Z, Y),
        out_shape=jax.ShapeDtypeStruct((2, 4, B, B), BF16),
        in_specs=[hbm, smem, hbm, smem, vmem],
        out_specs=vmem,
        scratch_shapes=[
            pltpu.VMEM((2, C, B, B), BF16),
            pltpu.VMEM((1, C, B, B), BF16),
            pltpu.VMEM((2 * X, C, B, B), BF16),
            pltpu.VMEM((X, HALF, B), BF16),
            pltpu.VMEM((X, UNIT - HALF, B), BF16),
            pltpu.VMEM((Z, UNIT, B), BF16),
            pltpu.VMEM((Y, X, piece, B), F32),
            pltpu.VMEM((Y, X, piece, B), BF16),
            pltpu.VMEM((Y, X, piece, B), BF16),
            pltpu.VMEM((2, far_y + 1, X, piece, B), BF16),
            pltpu.VMEM((2, far_y, X, piece, B), BF16),
            pltpu.VMEM((X, piece, B), BF16),
            pltpu.VMEM((TABLE, 128), I32),
            pltpu.SMEM((TABLE, 128), I32),
            pltpu.VMEM((Z, 8, 128), I32),
            pltpu.SMEM((Z, 8, 128), I32),
            dma((2, X - 1)), dma((2, X - 1)),
            dma((6,)), dma((6,)),
            dma((2, far, 2)), dma((2, far, 2)),
            dma((Y,)), dma((Y,)),
            dma((2, far_y, X)), dma((2, far_y, X)),
            dma((X - 1,)), dma((X - 1,)),
            dma((3 + Z,)),
        ],
        compiler_params=pltpu.CompilerParams(
            collective_id=0, has_side_effects=True, vmem_limit_bytes=56 * 1024 * 1024),
        cost_estimate=pl.CostEstimate(flops=2 * 128 * 4 * B * B * B, bytes_accessed=1 << 20, transcendentals=0),
    )(amplitudes, amplitude_mask, integrals, integral_mask, owners.reshape(1, -1))


def solution(mesh):
    Z, Y = mesh.shape["row"] // X, mesh.shape["col"] // 2
    return jax.shard_map(
        functools.partial(per_device, Z, Y),
        mesh=mesh,
        in_specs=(
            P("row", "col", None, None),
            P("row", "col"),
            P("row", "col", None, None),
            P("row", "col"),
            P(),
        ),
        out_specs=P("row", "col", None, None),
        check_vma=False,
    )
```

time: 94 us -> 80.1 us (0.85)
  Pallas kernels: 90.3 us -> 78.2 us
  local copies, waits for them, and re-layouts: 3.47 us -> 1.67 us
    pallas_call x1, Pallas kernels: 90.3 us -> 78.2 us  [per_device(): pl.pallas_call(functools.partial(kernel, Z, Y), out_shape=jax.ShapeDtypeS...]
    unnamed x10 -> x1, local copies, waits for them, and re-layouts: 3.47 us -> 1.67 us
where the time goes in v2:
time: 80.1 us; the launch traced here: 79.9 us
  Pallas kernels  78.2 us (98%)
  local copies, waits for them, and re-layouts  1.67 us (2%)
    pallas_call x1, Pallas kernels, per_device(): pl.pallas_call(functools.partial(kernel, Z, Y), out_shape=jax.ShapeDtypeS...  78.2 us
    unnamed x1, local copies, waits for them, and re-layouts  1.67 us

profile of v2, /device:TPU:1, one launch (start us, length us, event | category | flops | bytes accessed | tf_op | source)
XLA Modules:
  0.0 79.9 jit_solution(11825462032519465739)
XLA Ops:
  0.0 78.2 %shard_map.55 = bf16[2,4,128,128]{3,2,1,0:T(8,128)(2,1)} custom-call(bf16[2,8,128,128]{3,2,1,0:T(8,128)(2,1)} %amp_hbm.1, s32[2,8]{1,0:T(2,128)} %amp_mask.1, bf16[1,8,128,128]{3,2,1,0:T(8,128)(2,1)} %int_hbm.1, s32[1,8]{1,0:T(1,128)} %int_mask.1, s32[1,48]{1,0:T(1,128)} %bitcast.1), custom_call_target="tpu_custom_call" | custom-call | flops 2147483648 | bytes 1048576 | tf_op jit(solution)/shard_map/pallas_call | solution.py:354
  78.2 1.7 %copy.7 = bf16[2,4,128,128]{3,2,1,0:T(8,128)(2,1)} copy(bf16[2,4,128,128]{3,2,1,0:T(8,128)(2,1)} %shard_map.55) | data formatting | bytes 524288

commit v3 on v2

--- a/solution.py
+++ b/solution.py
@@ -98,7 +98,7 @@
 
 def kernel(
     Z, Y, amp_hbm, amp_mask, int_hbm, int_mask, owners, out,
-    amp, integral, A, XI0, XI1, G, mine, part_out, part_in, ring_out, ring_in, met, table_v, table_s, meta_v, meta_s,
+    amp, integral, A0, A1, A2, A3, XI0, XI1, G, partial, part_out, part_in, ring_out, ring_in, own_out, met, table_v, table_s, meta_v, meta_s,
     xi_send, xi_recv, a_send, a_recv, z_send, z_recv, p_send, p_recv, r_send, r_recv, m_send, m_recv, local,
 ):
     row, col = lax.axis_index("row"), lax.axis_index("col")
@@ -118,10 +118,14 @@
     def at_y(shift):
         return (row, ((y + shift) % Y) * 2 + core)
 
+    def at_xy(right, up):
+        return (z * X + (x + right) % X, ((y + up) % Y) * 2 + core)
+
     partner = (row, y * 2 + (1 - core))
 
     barrier = pltpu.get_barrier_semaphore()
     peers = [at_x(1), at_x(2), at_x(3), at_z(1), at_z(Z - 1), at_y(1), at_y(Y - 1), partner]
+    peers += [at_xy(r, up) for r in range(1, X) for up in (1, Y - 1)]
     for peer in peers:
         pl.semaphore_signal(barrier, inc=1, device_id=peer, device_id_type=pl.DeviceIdType.MESH)
 
@@ -162,19 +166,20 @@
     amp_in.wait()
     for i in range(2):
         for c in range(C):
-            A[i, c] = amp[i, c] * amp_mask[i, c].astype(F32).astype(BF16)
+            A0[i, c] = amp[i, c] * amp_mask[i, c].astype(F32).astype(BF16)
     for way in range(2):
         for r in LATE[1 - way]:
             ring_in[way, 0, r] = jnp.zeros_like(ring_in[way, 0, r])
 
+    A = (A0, A1, A2, A3)
     a_copies = [
-        copy(A.at[0], A.at[6], a_send.at[0], a_recv.at[0], at_x(1)),
-        copy(A.at[1], A.at[3], a_send.at[1], a_recv.at[1], at_x(3)),
-        copy(A.at[1], A.at[7], a_send.at[2], a_recv.at[2], at_x(1)),
-        copy(A.at[0], A.at[2], a_send.at[3], a_recv.at[3], at_x(3)),
+        copy(A0.at[0], A3.at[0], a_send.at[0], a_recv.at[0], at_x(1)),
+        copy(A0.at[1], A1.at[1], a_send.at[1], a_recv.at[1], at_x(3)),
+        copy(A0.at[1], A3.at[1], a_send.at[2], a_recv.at[2], at_x(1)),
+        copy(A0.at[0], A1.at[0], a_send.at[3], a_recv.at[3], at_x(3)),
     ]
-    a_on_right = copy(A.at[6], A.at[4], a_send.at[4], a_recv.at[4], at_x(1))
-    a_on_left = copy(A.at[3], A.at[5], a_send.at[5], a_recv.at[5], at_x(3))
+    a_on_right = copy(A3.at[0], A2.at[0], a_send.at[4], a_recv.at[4], at_x(1))
+    a_on_left = copy(A1.at[1], A2.at[1], a_send.at[5], a_recv.at[5], at_x(3))
 
     table_v[...] = table_of(owners[...], x, z, col, 2 * Y)
     table_copy = pltpu.make_async_copy(table_v, table_s, local.at[0])
@@ -203,11 +208,23 @@
     for c in a_copies:
         c.start()
 
+    def meta_copy(rel):
+        return pltpu.make_async_copy(meta_v.at[rel], meta_s.at[rel], local.at[1 + rel])
+
     def meta_out(rel):
         meta_v[rel] = G[rel, V * B:UNIT, :].astype(F32).astype(I32)[0:8]
-        pltpu.make_async_copy(meta_v.at[rel], meta_s.at[rel], local.at[1 + rel]).start()
+        meta_copy(rel).start()
+
+    def products(rel, pieces):
+        where = [jnp.clip(meta_s[rel, j, 0], 0, C - 1) for j in range(V)]
+        wide = jnp.concatenate([G[rel, j * B:(j + 1) * B, :] for j in range(V)], axis=1)
+        for r in pieces:
+            tiles = jnp.concatenate([A[r][:, where[j]].reshape(2 * B, B) for j in range(V)], axis=1)
+            total = lax.dot_general(tiles, wide, (((1,), (1,)), ((), ())), preferred_element_type=F32)
+            partial[rel, r] = total.astype(BF16)
 
     meta_out(0)
+    seen, crossed = [0], []
     for s in range(far - 1):
         for h in range(2):
             to_right[s][h].wait_recv()
@@ -220,20 +237,37 @@
                 to_left[s + 1][0].start()
         meta_out(Z - 1 - s)
         meta_out(s + 1)
-        if s == 2:
+        if s == far - 4:
             a_copies[0].wait_recv()
             a_on_right.start()
             a_copies[1].wait_recv()
             a_on_left.start()
+        if s == far - 3:
+            a_copies[2].wait_recv()
+            a_copies[3].wait_recv()
+        now = [0] if s == 0 else [Z - s, s]
+        for rel in now:
+            meta_copy(rel).wait()
+            products(rel, (0,))
+        if s >= far - 3:
+            for rel in [rel for rel in seen if rel not in crossed]:
+                products(rel, (1, 3))
+                crossed.append(rel)
+        seen += [Z - 1 - s, s + 1]
+    for rel in seen[-2:]:
+        meta_copy(rel).wait()
+        products(rel, (0,))
+    for rel in [rel for rel in seen if rel not in crossed]:
+        products(rel, (1, 3))
+    a_on_right.wait_recv()
+    a_on_left.wait_recv()
+    for rel in seen:
+        products(rel, (2,))
     to_right[far - 1][0].wait_recv()
     to_left[far - 1][0].wait_recv()
     meta_out(far)
-    a_copies[2].wait_recv()
-    a_copies[3].wait_recv()
-    a_on_right.wait_recv()
-    a_on_left.wait_recv()
-    for rel in range(Z):
-        pltpu.make_async_copy(meta_v.at[rel], meta_s.at[rel], local.at[1 + rel]).wait()
+    meta_copy(far).wait()
+    products(far, range(X))
 
     far_y = Y // 2
 
@@ -246,42 +280,51 @@
             at_y(1 if way == 0 else Y - 1),
         )
 
-    def products(n, slot_y):
-        for whose in (1, 0):
-            owner = slot_y * 2 + (core + whose) % 2
-            named = table_s[owner, 0]
-            filled = jnp.where(named > 0, 1.0, 0.0).astype(F32)
-            rel = jnp.clip(named - 1, 0, Z - 1) - z
-            rel = jnp.where(rel < 0, rel + Z, rel)
-            where = [jnp.clip(meta_s[rel, j, 0], 0, C - 1) for j in range(V)]
-            unit = G[rel, 0:V * B, :]
-            wide = jnp.concatenate([unit[j * B:(j + 1) * B] for j in range(V)], axis=1)
-            for r in range(X):
-                tiles = jnp.concatenate([A[2 * r:2 * r + 2, where[j]].reshape(2 * B, B) for j in range(V)], axis=1)
-                total = filled * lax.dot_general(tiles, wide, (((1,), (1,)), ((), ())), preferred_element_type=F32)
-                if whose == 0:
-                    mine[n, r] = total
-                else:
-                    part_out[n, r] = total.astype(BF16)
-            if whose == 1:
-                part_copy(n).start()
-
-    def one(way, s):
-        products(2 * s + way, (y + (far_y - s if way == 0 else far_y + s)) % Y)
-
-    products(0, (y + far_y) % Y)
-    one(0, 1)
+    def slot_of(n):
+        if isinstance(n, int) and n < 2:
+            return (y + far_y) % Y if n == 0 else y
+        s, way = n // 2, n % 2
+        return (y + far_y + (2 * way - 1) * s + Y) % Y
+
+    def source_of(n, whose):
+        named = table_s[slot_of(n) * 2 + (core + whose) % 2, 0]
+        rel = jnp.clip(named - 1, 0, Z - 1) - z
+        return jnp.where(rel < 0, rel + Z, rel), jnp.where(named > 0, 1.0, 0.0).astype(F32)
+
+    def stage(n):
+        rel, filled = source_of(n, 1)
+        part_out[n] = partial[rel] * filled.astype(BF16)
+        part_copy(n).start()
+
+    stage(0)
+    stage(2)
+    stage(3)
+    rel_0, filled_0 = source_of(0, 0)
     part_copy(0).wait_recv()
     for k in range(2):
         for way in range(2):
             r = LATE[way][k]
-            ring_out[way, 0, r] = (mine[0, r] + part_in[0, r].astype(F32)).astype(BF16)
+            ring_out[way, 0, r] = (partial[rel_0, r].astype(F32) * filled_0 + part_in[0, r].astype(F32)).astype(BF16)
             ring_copy(0, way, r).start()
-    one(1, 1)
+    for n in (*range(4, Y), 1):
+        stage(n)
+
+    def last_copy(way, r):
+        if way == 2:
+            source, to = own_out.at[r], at_x(r)
+        else:
+            source, to = ring_out.at[way, far_y - 1, r], at_xy(r, 1 if way == 0 else Y - 1)
+        return copy(source, met.at[way, (X - r) % X], m_send.at[way, r], m_recv.at[way, r], to)
+
+    def ring_sums(s, way, r, source):
+        rel, filled = source
+        own = partial[rel, r].astype(F32) * filled
+        return (own + part_in[2 * s + way, r].astype(F32) + ring_in[way, s - 1, r].astype(F32)).astype(BF16)
 
     def ring_step(s, carry):
         part_copy(2 * s).wait_recv()
         part_copy(2 * s + 1).wait_recv()
+        sources = [source_of(2 * s + way, 0) for way in range(2)]
         for way, r in ORDER:
             if r in LATE[way]:
                 ring_copy(s - 1, way, r).wait_recv()
@@ -289,45 +332,28 @@
                 @pl.when(s > 1)
                 def _():
                     ring_copy(s - 1, way, r).wait_recv()
-            n = 2 * s + way
-            total = mine[n, r] + part_in[n, r].astype(F32) + ring_in[way, s - 1, r].astype(F32)
-            ring_out[way, s, r] = total.astype(BF16)
+            ring_out[way, s, r] = ring_sums(s, way, r, sources[way])
             ring_copy(s, way, r).start()
-
-        @pl.when(s < far_y - 1)
-        def _():
-            one(0, s + 1)
-            one(1, s + 1)
         return carry
 
-    lax.fori_loop(1, far_y, ring_step, jnp.int32(0))
-    products(1, y)
-
-    def met_copy(r):
-        return copy(ring_out.at[0, far_y, r], met.at[X - r], m_send.at[r - 1], m_recv.at[r - 1], at_x(r))
-
     last = far_y - 1
+    lax.fori_loop(1, last, ring_step, jnp.int32(0))
     part_copy(1).wait_recv()
+    rel_1, filled_1 = source_of(1, 0)
+    for r in (2, 1, 3, 0):
+        sums = (partial[rel_1, r].astype(F32) * filled_1 + part_in[1, r].astype(F32)).astype(BF16)
+        if r == 0:
+            met[2, 0] = sums
+        else:
+            own_out[r] = sums
+            last_copy(2, r).start()
+    part_copy(2 * last).wait_recv()
+    part_copy(2 * last + 1).wait_recv()
+    sources = [source_of(2 * last + way, 0) for way in range(2)]
     for way, r in ORDER:
-        ring_copy(last, way, r).wait_recv()
-        if r in LATE[way]:
-            total = (mine[1, r] + part_in[1, r].astype(F32)) + (
-                ring_in[0, last, r].astype(F32) + ring_in[1, last, r].astype(F32))
-            if r == 0:
-                met[0] = total.astype(BF16)
-            else:
-                ring_out[0, far_y, r] = total.astype(BF16)
-                met_copy(r).start()
-    for r in range(1, X):
-        met_copy(r).wait_recv()
-    slots = out.shape[1]
-    for t in range(slots):
-        named = table_s[2 * Y + t, 0]
-        filled = jnp.where(named > 0, 1.0, 0.0).astype(BF16)
-        rel = jnp.clip(named - 1, 0, X - 1) - x
-        tiles = met[jnp.where(rel < 0, rel + X, rel)] * filled
-        for i in range(2):
-            out[i, t] = tiles[i * B:(i + 1) * B]
+        ring_copy(last - 1, way, r).wait_recv()
+        ring_out[way, last, r] = ring_sums(last, way, r, sources[way])
+        last_copy(way, r).start()
 
     for c in [*xi_copies[0], *xi_copies[1], *a_copies, a_on_right, a_on_left]:
         c.wait_send()
@@ -336,12 +362,29 @@
             c.wait_send()
     for n in range(Y):
         part_copy(n).wait_send()
-    for s in range(far_y):
+    for s in range(last):
         for way, r in ORDER:
             if s > 0 or r in LATE[way]:
                 ring_copy(s, way, r).wait_send()
+
     for r in range(1, X):
-        met_copy(r).wait_send()
+        last_copy(2, r).wait_recv()
+    for way, r in ORDER:
+        last_copy(way, r).wait_recv()
+    slots = out.shape[1]
+    for t in range(slots):
+        named = table_s[2 * Y + t, 0]
+        filled = jnp.where(named > 0, 1.0, 0.0).astype(F32)
+        rel = jnp.clip(named - 1, 0, X - 1) - x
+        rel = jnp.where(rel < 0, rel + X, rel)
+        tiles = (filled * (met[0, rel].astype(F32) + met[1, rel].astype(F32) + met[2, rel].astype(F32))).astype(BF16)
+        for i in range(2):
+            out[i, t] = tiles[i * B:(i + 1) * B]
+
+    for r in range(1, X):
+        last_copy(2, r).wait_send()
+    for way, r in ORDER:
+        last_copy(way, r).wait_send()
 
 
 def per_device(Z, Y, amplitudes, amplitude_mask, integrals, integral_mask, owners):
@@ -359,16 +402,17 @@
         scratch_shapes=[
             pltpu.VMEM((2, C, B, B), BF16),
             pltpu.VMEM((1, C, B, B), BF16),
-            pltpu.VMEM((2 * X, C, B, B), BF16),
+            *[pltpu.VMEM((2, C, B, B), BF16)] * X,
             pltpu.VMEM((X, HALF, B), BF16),
             pltpu.VMEM((X, UNIT - HALF, B), BF16),
             pltpu.VMEM((Z, UNIT, B), BF16),
-            pltpu.VMEM((Y, X, piece, B), F32),
+            pltpu.VMEM((Z, X, piece, B), BF16),
             pltpu.VMEM((Y, X, piece, B), BF16),
             pltpu.VMEM((Y, X, piece, B), BF16),
-            pltpu.VMEM((2, far_y + 1, X, piece, B), BF16),
             pltpu.VMEM((2, far_y, X, piece, B), BF16),
+            pltpu.VMEM((2, far_y - 1, X, piece, B), BF16),
             pltpu.VMEM((X, piece, B), BF16),
+            pltpu.VMEM((3, X, piece, B), BF16),
             pltpu.VMEM((TABLE, 128), I32),
             pltpu.SMEM((TABLE, 128), I32),
             pltpu.VMEM((Z, 8, 128), I32),
@@ -377,8 +421,8 @@
             dma((6,)), dma((6,)),
             dma((2, far, 2)), dma((2, far, 2)),
             dma((Y,)), dma((Y,)),
-            dma((2, far_y, X)), dma((2, far_y, X)),
-            dma((X - 1,)), dma((X - 1,)),
+            dma((2, far_y - 1, X)), dma((2, far_y - 1, X)),
+            dma((3, X)), dma((3, X)),
             dma((3 + Z,)),
         ],
         compiler_params=pltpu.CompilerParams(

time: 80.1 us -> 76.7 us (0.958)
  Pallas kernels: 78.2 us -> 74.9 us
    pallas_call x1, Pallas kernels: 78.2 us -> 74.9 us  [per_device(): pl.pallas_call(functools.partial(kernel, Z, Y), out_shape=jax.ShapeDtypeS...]
where the time goes in v3:
time: 76.7 us; the launch traced here: 76.6 us
  Pallas kernels  74.9 us (98%)
  local copies, waits for them, and re-layouts  1.67 us (2%)
    pallas_call x1, Pallas kernels, per_device(): pl.pallas_call(functools.partial(kernel, Z, Y), out_shape=jax.ShapeDtypeS...  74.9 us
    unnamed x1, local copies, waits for them, and re-layouts  1.67 us

profile of v3, /device:TPU:1, one launch (start us, length us, event | category | flops | bytes accessed | tf_op | source)
XLA Modules:
  0.0 76.6 jit_solution(6190469739701665743)
XLA Ops:
  0.0 74.9 %shard_map.55 = bf16[2,4,128,128]{3,2,1,0:T(8,128)(2,1)} custom-call(bf16[2,8,128,128]{3,2,1,0:T(8,128)(2,1)} %amp_hbm.1, s32[2,8]{1,0:T(2,128)} %amp_mask.1, bf16[1,8,128,128]{3,2,1,0:T(8,128)(2,1)} %int_hbm.1, s32[1,8]{1,0:T(1,128)} %int_mask.1, s32[1,48]{1,0:T(1,128)} %bitcast.1), custom_call_target="tpu_custom_call" | custom-call | flops 2147483648 | bytes 1048576 | tf_op jit(solution)/shard_map/pallas_call | solution.py:397
  74.9 1.7 %copy.7 = bf16[2,4,128,128]{3,2,1,0:T(8,128)(2,1)} copy(bf16[2,4,128,128]{3,2,1,0:T(8,128)(2,1)} %shard_map.55) | data formatting | bytes 524288

commit v4 on v3

--- a/solution.py
+++ b/solution.py
@@ -14,7 +14,7 @@
 V = 4
 META = 16
 UNIT = V * B + META
-HALF = 256
+PARTS = [(0, META + B)] + [(META + j * B, B) for j in range(1, V)]
 F32 = jnp.float32
 BF16 = jnp.bfloat16
 I32 = jnp.int32
@@ -98,16 +98,11 @@
 
 def kernel(
     Z, Y, amp_hbm, amp_mask, int_hbm, int_mask, owners, out,
-    amp, integral, A0, A1, A2, A3, XI0, XI1, G, partial, part_out, part_in, ring_out, ring_in, own_out, met, table_v, table_s, meta_v, meta_s,
-    xi_send, xi_recv, a_send, a_recv, z_send, z_recv, p_send, p_recv, r_send, r_recv, m_send, m_recv, local,
+    amp, integral, A0, A1, A2, A3, XI0, XI1, XI2, XI3, G, partial, part_out, part_in, ring_out, ring_in, own_out, met, table_v, table_s, meta_v, meta_s,
+    xi_send, xi_recv, a_send, a_recv, z_send, z_recv, f_send, f_recv, p_send, p_recv, r_send, r_recv, m_send, m_recv, local,
 ):
     row, col = lax.axis_index("row"), lax.axis_index("col")
     x, z, y, core = row % X, row // X, col // 2, col % 2
-
-    int_in = pltpu.make_async_copy(int_hbm, integral, local.at[Z + 1])
-    amp_in = pltpu.make_async_copy(amp_hbm, amp, local.at[Z + 2])
-    int_in.start()
-    amp_in.start()
 
     def at_x(shift):
         return (z * X + (x + shift) % X, col)
@@ -128,6 +123,11 @@
     peers += [at_xy(r, up) for r in range(1, X) for up in (1, Y - 1)]
     for peer in peers:
         pl.semaphore_signal(barrier, inc=1, device_id=peer, device_id_type=pl.DeviceIdType.MESH)
+
+    int_in = pltpu.make_async_copy(int_hbm, integral, local.at[Z + 1])
+    amp_in = pltpu.make_async_copy(amp_hbm, amp, local.at[Z + 2])
+    int_in.start()
+    amp_in.start()
 
     def copy(src, dst, send, recv, to):
         return pltpu.make_async_remote_copy(
@@ -142,24 +142,28 @@
         for j in range(V):
             places[j] = jnp.where((kept[c] != 0) & (before == j), c, places[j])
         before = before + kept[c]
-    XI = (XI0, XI1)
-    for j in range(V):
-        scale = jnp.where(before > j, 1.0, 0.0).astype(BF16)
-        XI[j // 2][0, (j % 2) * B:(j % 2 + 1) * B, :] = integral[0, places[j]] * scale
+    XI = (XI0, XI1, XI2, XI3)
     at = lax.broadcasted_iota(I32, (META, B), 0)
     meta = jnp.zeros((META, B), I32)
     for j in range(V):
         meta = jnp.where(at == j, places[j], meta)
-    XI1[0, V * B - HALF:UNIT - HALF, :] = meta.astype(F32).astype(BF16)
+    XI0[0, 0:META] = meta.astype(F32).astype(BF16)
+    for j in range(V):
+        scale = jnp.where(before > j, 1.0, 0.0).astype(BF16)
+        first = META if j == 0 else 0
+        XI[j][0, first:first + B] = integral[0, places[j]] * scale
 
     pl.semaphore_wait(barrier, len(peers))
 
-    PARTS = (pl.ds(0, HALF), pl.ds(HALF, UNIT - HALF))
     xi_copies = [
-        [copy(XI[h].at[0], XI[h].at[X - r], xi_send.at[h, r - 1], xi_recv.at[h, r - 1], at_x(r)) for r in (2, 1, 3)]
-        for h in range(2)
+        [copy(XI[h].at[0], XI[h].at[X - r], xi_send.at[h], xi_recv.at[h], at_x(r)) for r in (2, 1, 3)]
+        for h in range(V)
     ]
-    for h in range(2):
+
+    def xi_all(h):
+        return copy(XI[h].at[1:X], XI[h].at[1:X], xi_send.at[h], xi_recv.at[h], at_x(1))
+
+    for h in range(V):
         for c in xi_copies[h]:
             c.start()
 
@@ -167,42 +171,43 @@
     for i in range(2):
         for c in range(C):
             A0[i, c] = amp[i, c] * amp_mask[i, c].astype(F32).astype(BF16)
-    for way in range(2):
-        for r in LATE[1 - way]:
-            ring_in[way, 0, r] = jnp.zeros_like(ring_in[way, 0, r])
 
     A = (A0, A1, A2, A3)
     a_copies = [
         copy(A0.at[0], A3.at[0], a_send.at[0], a_recv.at[0], at_x(1)),
-        copy(A0.at[1], A1.at[1], a_send.at[1], a_recv.at[1], at_x(3)),
-        copy(A0.at[1], A3.at[1], a_send.at[2], a_recv.at[2], at_x(1)),
-        copy(A0.at[0], A1.at[0], a_send.at[3], a_recv.at[3], at_x(3)),
+        copy(A0.at[1], A1.at[1], a_send.at[0], a_recv.at[1], at_x(3)),
+        copy(A0.at[1], A3.at[1], a_send.at[1], a_recv.at[2], at_x(1)),
+        copy(A0.at[0], A1.at[0], a_send.at[1], a_recv.at[3], at_x(3)),
     ]
-    a_on_right = copy(A3.at[0], A2.at[0], a_send.at[4], a_recv.at[4], at_x(1))
-    a_on_left = copy(A1.at[1], A2.at[1], a_send.at[5], a_recv.at[5], at_x(3))
+    a_on_right = copy(A3.at[0], A2.at[0], a_send.at[2], a_recv.at[4], at_x(1))
+    a_on_left = copy(A1.at[1], A2.at[1], a_send.at[2], a_recv.at[5], at_x(3))
 
     table_v[...] = table_of(owners[...], x, z, col, 2 * Y)
     table_copy = pltpu.make_async_copy(table_v, table_s, local.at[0])
     table_copy.start()
 
     far = Z // 2
+    RIGHT, LEFT = range(0, V // 2), range(V // 2, V)
+
+    def rows_of(h):
+        return pl.ds(*PARTS[h])
+
     to_right = [
-        [copy(G.at[(Z - s) % Z, rows], G.at[Z - 1 - s, rows], z_send.at[0, s, h], z_recv.at[0, s, h], at_z(1))
-         for h, rows in enumerate(PARTS) if s < far - 1 or h == 0]
+        {h: copy(G.at[(Z - s) % Z, rows_of(h)], G.at[Z - 1 - s, rows_of(h)], z_send.at[0, s // (far - 1)], z_recv.at[0, s, h], at_z(1))
+         for h in (range(V) if s < far - 1 else RIGHT)}
         for s in range(far)
     ]
     to_left = [
-        [copy(G.at[s, rows], G.at[s + 1, rows], z_send.at[1, s, h], z_recv.at[1, s, h], at_z(Z - 1))
-         for h, rows in enumerate(PARTS) if s < far - 1 or h == 1]
+        {h: copy(G.at[s, rows_of(h)], G.at[s + 1, rows_of(h)], z_send.at[1, s // (far - 1)], z_recv.at[1, s, h], at_z(Z - 1))
+         for h in (range(V) if s < far - 1 else LEFT)}
         for s in range(far)
     ]
 
     table_copy.wait()
     from_rel = (jnp.clip(table_s[2 * Y + 8, 0], 0, X - 1) - x + X) % X
-    for h, rows in enumerate(PARTS):
-        for c in xi_copies[h]:
-            c.wait_recv()
-        G[0, rows] = XI[h][from_rel]
+    for h in range(V):
+        xi_all(h).wait_recv()
+        G[0, rows_of(h)] = XI[h][from_rel]
         to_right[0][h].start()
         to_left[0][h].start()
     for c in a_copies:
@@ -212,12 +217,12 @@
         return pltpu.make_async_copy(meta_v.at[rel], meta_s.at[rel], local.at[1 + rel])
 
     def meta_out(rel):
-        meta_v[rel] = G[rel, V * B:UNIT, :].astype(F32).astype(I32)[0:8]
+        meta_v[rel] = G[rel, 0:META, :].astype(F32).astype(I32)[0:8]
         meta_copy(rel).start()
 
     def products(rel, pieces):
         where = [jnp.clip(meta_s[rel, j, 0], 0, C - 1) for j in range(V)]
-        wide = jnp.concatenate([G[rel, j * B:(j + 1) * B, :] for j in range(V)], axis=1)
+        wide = jnp.concatenate([G[rel, META + j * B:META + (j + 1) * B, :] for j in range(V)], axis=1)
         for r in pieces:
             tiles = jnp.concatenate([A[r][:, where[j]].reshape(2 * B, B) for j in range(V)], axis=1)
             total = lax.dot_general(tiles, wide, (((1,), (1,)), ((), ())), preferred_element_type=F32)
@@ -226,15 +231,11 @@
     meta_out(0)
     seen, crossed = [0], []
     for s in range(far - 1):
-        for h in range(2):
-            to_right[s][h].wait_recv()
-            if s + 1 < far - 1 or h == 0:
-                to_right[s + 1][h].start()
-            to_left[s][h].wait_recv()
-            if s + 1 < far - 1:
-                to_left[s + 1][h].start()
-            elif h == 1:
-                to_left[s + 1][0].start()
+        for h in range(V):
+            for chain in (to_right, to_left):
+                chain[s][h].wait_recv()
+                if h in chain[s + 1]:
+                    chain[s + 1][h].start()
         meta_out(Z - 1 - s)
         meta_out(s + 1)
         if s == far - 4:
@@ -263,20 +264,25 @@
     a_on_left.wait_recv()
     for rel in seen:
         products(rel, (2,))
-    to_right[far - 1][0].wait_recv()
-    to_left[far - 1][0].wait_recv()
-    meta_out(far)
+    for chain in (to_right, to_left):
+        for h, c in chain[far - 1].items():
+            c.wait_recv()
+            if h == 0:
+                meta_out(far)
     meta_copy(far).wait()
     products(far, range(X))
 
     far_y = Y // 2
 
+    def piece_copy(r):
+        return copy(part_out.at[0, r], part_in.at[0, r], f_send.at[0], f_recv.at[r], partner)
+
     def part_copy(n):
-        return copy(part_out.at[n], part_in.at[n], p_send.at[n], p_recv.at[n], partner)
+        return copy(part_out.at[n], part_in.at[n], p_send.at[0], p_recv.at[n], partner)
 
     def ring_copy(s, way, r):
         return copy(
-            ring_out.at[way, s, r], ring_in.at[way, s, r], r_send.at[way, s, r], r_recv.at[way, s, r],
+            ring_out.at[way, s, r], ring_in.at[way, s, r], r_send.at[0 if s == 0 else 1 + way], r_recv.at[way, s, r],
             at_y(1 if way == 0 else Y - 1),
         )
 
@@ -296,14 +302,17 @@
         part_out[n] = partial[rel] * filled.astype(BF16)
         part_copy(n).start()
 
-    stage(0)
+    rel, filled = source_of(0, 1)
+    for r in (2, 1, 0, 3):
+        part_out[0, r] = partial[rel, r] * filled.astype(BF16)
+        piece_copy(r).start()
+    rel_0, filled_0 = source_of(0, 0)
     stage(2)
     stage(3)
-    rel_0, filled_0 = source_of(0, 0)
-    part_copy(0).wait_recv()
     for k in range(2):
         for way in range(2):
             r = LATE[way][k]
+            piece_copy(r).wait_recv()
             ring_out[way, 0, r] = (partial[rel_0, r].astype(F32) * filled_0 + part_in[0, r].astype(F32)).astype(BF16)
             ring_copy(0, way, r).start()
     for n in (*range(4, Y), 1):
@@ -314,30 +323,31 @@
             source, to = own_out.at[r], at_x(r)
         else:
             source, to = ring_out.at[way, far_y - 1, r], at_xy(r, 1 if way == 0 else Y - 1)
-        return copy(source, met.at[way, (X - r) % X], m_send.at[way, r], m_recv.at[way, r], to)
+        return copy(source, met.at[way, (X - r) % X], m_send.at[way], m_recv.at[way], to)
 
     def ring_sums(s, way, r, source):
         rel, filled = source
         own = partial[rel, r].astype(F32) * filled
-        return (own + part_in[2 * s + way, r].astype(F32) + ring_in[way, s - 1, r].astype(F32)).astype(BF16)
-
-    def ring_step(s, carry):
+        sums = own + part_in[2 * s + way, r].astype(F32)
+        if s > 1 or r in LATE[way]:
+            sums = sums + ring_in[way, s - 1, r].astype(F32)
+        return sums.astype(BF16)
+
+    def ring_step(s):
         part_copy(2 * s).wait_recv()
         part_copy(2 * s + 1).wait_recv()
         sources = [source_of(2 * s + way, 0) for way in range(2)]
         for way, r in ORDER:
             if r in LATE[way]:
                 ring_copy(s - 1, way, r).wait_recv()
-            else:
-                @pl.when(s > 1)
-                def _():
-                    ring_copy(s - 1, way, r).wait_recv()
+            elif s > 1:
+                ring_copy(s - 1, way, r).wait_recv()
             ring_out[way, s, r] = ring_sums(s, way, r, sources[way])
             ring_copy(s, way, r).start()
-        return carry
 
     last = far_y - 1
-    lax.fori_loop(1, last, ring_step, jnp.int32(0))
+    for s in range(1, last):
+        ring_step(s)
     part_copy(1).wait_recv()
     rel_1, filled_1 = source_of(1, 0)
     for r in (2, 1, 3, 0):
@@ -355,22 +365,28 @@
         ring_out[way, last, r] = ring_sums(last, way, r, sources[way])
         last_copy(way, r).start()
 
-    for c in [*xi_copies[0], *xi_copies[1], *a_copies, a_on_right, a_on_left]:
-        c.wait_send()
-    for s in range(far):
-        for c in to_right[s] + to_left[s]:
-            c.wait_send()
-    for n in range(Y):
-        part_copy(n).wait_send()
-    for s in range(last):
-        for way, r in ORDER:
-            if s > 0 or r in LATE[way]:
-                ring_copy(s, way, r).wait_send()
-
-    for r in range(1, X):
-        last_copy(2, r).wait_recv()
-    for way, r in ORDER:
-        last_copy(way, r).wait_recv()
+    def left(ref, sem):
+        copy(ref, ref, sem, f_recv.at[0], partner).wait_send()
+
+    for h in range(V):
+        xi_all(h).wait_send()
+    for k in range(3):
+        left(A0, a_send.at[k])
+    for chain, side in ((to_right, 0), (to_left, 1)):
+        left(G.at[0:far - 1], z_send.at[side, 0])
+        left(G.at[0, 0:sum(PARTS[h][1] for h in chain[far - 1])], z_send.at[side, 1])
+    left(part_out.at[0], f_send.at[0])
+    left(part_out.at[1:Y], p_send.at[0])
+    left(ring_out.at[0, 0], r_send.at[0])
+    for way in range(2):
+        left(ring_out.at[way, 1:last], r_send.at[1 + way])
+
+    def met_all(way):
+        ref = met.at[way] if way < 2 else met.at[2, 1:X]
+        return copy(ref, ref, m_send.at[way], m_recv.at[way], partner)
+
+    for way in (2, 0, 1):
+        met_all(way).wait_recv()
     slots = out.shape[1]
     for t in range(slots):
         named = table_s[2 * Y + t, 0]
@@ -381,10 +397,8 @@
         for i in range(2):
             out[i, t] = tiles[i * B:(i + 1) * B]
 
-    for r in range(1, X):
-        last_copy(2, r).wait_send()
-    for way, r in ORDER:
-        last_copy(way, r).wait_send()
+    for way in range(3):
+        met_all(way).wait_send()
 
 
 def per_device(Z, Y, amplitudes, amplitude_mask, integrals, integral_mask, owners):
@@ -403,8 +417,7 @@
             pltpu.VMEM((2, C, B, B), BF16),
             pltpu.VMEM((1, C, B, B), BF16),
             *[pltpu.VMEM((2, C, B, B), BF16)] * X,
-            pltpu.VMEM((X, HALF, B), BF16),
-            pltpu.VMEM((X, UNIT - HALF, B), BF16),
+            *[pltpu.VMEM((X, rows, B), BF16) for _, rows in PARTS],
             pltpu.VMEM((Z, UNIT, B), BF16),
             pltpu.VMEM((Z, X, piece, B), BF16),
             pltpu.VMEM((Y, X, piece, B), BF16),
@@ -417,12 +430,13 @@
             pltpu.SMEM((TABLE, 128), I32),
             pltpu.VMEM((Z, 8, 128), I32),
             pltpu.SMEM((Z, 8, 128), I32),
-            dma((2, X - 1)), dma((2, X - 1)),
-            dma((6,)), dma((6,)),
-            dma((2, far, 2)), dma((2, far, 2)),
-            dma((Y,)), dma((Y,)),
-            dma((2, far_y - 1, X)), dma((2, far_y - 1, X)),
-            dma((3, X)), dma((3, X)),
+            dma((V,)), dma((V,)),
+            dma((3,)), dma((6,)),
+            dma((2, 2)), dma((2, far, V)),
+            dma((1,)), dma((X,)),
+            dma((1,)), dma((Y,)),
+            dma((3,)), dma((2, far_y - 1, X)),
+            dma((3,)), dma((3,)),
             dma((3 + Z,)),
         ],
         compiler_params=pltpu.CompilerParams(

time: 76.7 us -> 74.5 us (0.971)
  Pallas kernels: 74.9 us -> 72.7 us
    pallas_call x1, Pallas kernels: 74.9 us -> 72.7 us  [per_device(): pl.pallas_call(functools.partial(kernel, Z, Y), out_shape=jax.ShapeDtypeS...]
where the time goes in v4:
time: 74.5 us; the launch traced here: 74.4 us
  Pallas kernels  72.7 us (98%)
  local copies, waits for them, and re-layouts  1.67 us (2%)
    pallas_call x1, Pallas kernels, per_device(): pl.pallas_call(functools.partial(kernel, Z, Y), out_shape=jax.ShapeDtypeS...  72.7 us
    unnamed x1, local copies, waits for them, and re-layouts  1.67 us

profile of v4, /device:TPU:1, one launch (start us, length us, event | category | flops | bytes accessed | tf_op | source)
XLA Modules:
  0.0 74.4 jit_solution(3748572902669426718)
XLA Ops:
  0.0 72.7 %shard_map.55 = bf16[2,4,128,128]{3,2,1,0:T(8,128)(2,1)} custom-call(bf16[2,8,128,128]{3,2,1,0:T(8,128)(2,1)} %amp_hbm.1, s32[2,8]{1,0:T(2,128)} %amp_mask.1, bf16[1,8,128,128]{3,2,1,0:T(8,128)(2,1)} %int_hbm.1, s32[1,8]{1,0:T(1,128)} %int_mask.1, s32[1,48]{1,0:T(1,128)} %bitcast.1), custom_call_target="tpu_custom_call" | custom-call | flops 2147483648 | bytes 1048576 | tf_op jit(solution)/shard_map/pallas_call | solution.py:411
  72.7 1.7 %copy.7 = bf16[2,4,128,128]{3,2,1,0:T(8,128)(2,1)} copy(bf16[2,4,128,128]{3,2,1,0:T(8,128)(2,1)} %shard_map.55) | data formatting | bytes 524288

commit v5 on v4

--- a/solution.py
+++ b/solution.py
@@ -156,7 +156,7 @@
     pl.semaphore_wait(barrier, len(peers))
 
     xi_copies = [
-        [copy(XI[h].at[0], XI[h].at[X - r], xi_send.at[h], xi_recv.at[h], at_x(r)) for r in (2, 1, 3)]
+        [copy(XI[h].at[0], XI[h].at[X - r], xi_send.at[h], xi_recv.at[h], at_x(r)) for r in (1, 3, 2)]
         for h in range(V)
     ]
 
@@ -307,15 +307,13 @@
         part_out[0, r] = partial[rel, r] * filled.astype(BF16)
         piece_copy(r).start()
     rel_0, filled_0 = source_of(0, 0)
-    stage(2)
-    stage(3)
     for k in range(2):
         for way in range(2):
             r = LATE[way][k]
             piece_copy(r).wait_recv()
             ring_out[way, 0, r] = (partial[rel_0, r].astype(F32) * filled_0 + part_in[0, r].astype(F32)).astype(BF16)
             ring_copy(0, way, r).start()
-    for n in (*range(4, Y), 1):
+    for n in (2, 3, *range(4, Y), 1):
         stage(n)
 
     def last_copy(way, r):

time: 74.5 us -> 74.3 us (level)
  no operation moved by 1% of the time
where the time goes in v5:
time: 74.3 us; the launch traced here: 74.1 us
  Pallas kernels  72.4 us (97%)
  local copies, waits for them, and re-layouts  1.67 us (2%)
    pallas_call x1, Pallas kernels, per_device(): pl.pallas_call(functools.partial(kernel, Z, Y), out_shape=jax.ShapeDtypeS...  72.4 us
    unnamed x1, local copies, waits for them, and re-layouts  1.67 us

profile of v5, /device:TPU:1, one launch (start us, length us, event | category | flops | bytes accessed | tf_op | source)
XLA Modules:
  0.0 74.1 jit_solution(10685781187863575612)
XLA Ops:
  0.0 72.4 %shard_map.55 = bf16[2,4,128,128]{3,2,1,0:T(8,128)(2,1)} custom-call(bf16[2,8,128,128]{3,2,1,0:T(8,128)(2,1)} %amp_hbm.1, s32[2,8]{1,0:T(2,128)} %amp_mask.1, bf16[1,8,128,128]{3,2,1,0:T(8,128)(2,1)} %int_hbm.1, s32[1,8]{1,0:T(1,128)} %int_mask.1, s32[1,48]{1,0:T(1,128)} %bitcast.1), custom_call_target="tpu_custom_call" | custom-call | flops 2147483648 | bytes 1048576 | tf_op jit(solution)/shard_map/pallas_call | solution.py:409
  72.4 1.7 %copy.7 = bf16[2,4,128,128]{3,2,1,0:T(8,128)(2,1)} copy(bf16[2,4,128,128]{3,2,1,0:T(8,128)(2,1)} %shard_map.55) | data formatting | bytes 524288

commit v6 on v5

--- a/solution.py
+++ b/solution.py
@@ -92,8 +92,7 @@
 
 
 LATE = ((2, 0), (1, 3))
-ORDER = [(way, LATE[1 - way][k] if early else LATE[way][k])
-         for early in (True, False) for k in range(2) for way in range(2)]
+SPOT = {2: 0, 0: 1, 1: 2, 3: 3}
 
 
 def kernel(
@@ -280,11 +279,11 @@
     def part_copy(n):
         return copy(part_out.at[n], part_in.at[n], p_send.at[0], p_recv.at[n], partner)
 
-    def ring_copy(s, way, r):
+    def ring_copy(s, way, group):
+        pieces = pl.ds(2 * group, 2)
         return copy(
-            ring_out.at[way, s, r], ring_in.at[way, s, r], r_send.at[0 if s == 0 else 1 + way], r_recv.at[way, s, r],
-            at_y(1 if way == 0 else Y - 1),
-        )
+            ring_out.at[way, s, pieces], ring_in.at[way, s, pieces], r_send.at[0 if s == 0 else 1 + way],
+            r_recv.at[way, s, group], at_y(1 if way == 0 else Y - 1))
 
     def slot_of(n):
         if isinstance(n, int) and n < 2:
@@ -307,12 +306,12 @@
         part_out[0, r] = partial[rel, r] * filled.astype(BF16)
         piece_copy(r).start()
     rel_0, filled_0 = source_of(0, 0)
-    for k in range(2):
-        for way in range(2):
-            r = LATE[way][k]
+    for way in range(2):
+        for r in LATE[way]:
             piece_copy(r).wait_recv()
-            ring_out[way, 0, r] = (partial[rel_0, r].astype(F32) * filled_0 + part_in[0, r].astype(F32)).astype(BF16)
-            ring_copy(0, way, r).start()
+            ring_out[way, 0, SPOT[r]] = (
+                partial[rel_0, r].astype(F32) * filled_0 + part_in[0, r].astype(F32)).astype(BF16)
+        ring_copy(0, way, way).start()
     for n in (2, 3, *range(4, Y), 1):
         stage(n)
 
@@ -320,7 +319,7 @@
         if way == 2:
             source, to = own_out.at[r], at_x(r)
         else:
-            source, to = ring_out.at[way, far_y - 1, r], at_xy(r, 1 if way == 0 else Y - 1)
+            source, to = ring_out.at[way, far_y - 1, SPOT[r]], at_xy(r, 1 if way == 0 else Y - 1)
         return copy(source, met.at[way, (X - r) % X], m_send.at[way], m_recv.at[way], to)
 
     def ring_sums(s, way, r, source):
@@ -328,20 +327,21 @@
         own = partial[rel, r].astype(F32) * filled
         sums = own + part_in[2 * s + way, r].astype(F32)
         if s > 1 or r in LATE[way]:
-            sums = sums + ring_in[way, s - 1, r].astype(F32)
+            sums = sums + ring_in[way, s - 1, SPOT[r]].astype(F32)
         return sums.astype(BF16)
 
     def ring_step(s):
         part_copy(2 * s).wait_recv()
         part_copy(2 * s + 1).wait_recv()
         sources = [source_of(2 * s + way, 0) for way in range(2)]
-        for way, r in ORDER:
-            if r in LATE[way]:
-                ring_copy(s - 1, way, r).wait_recv()
-            elif s > 1:
-                ring_copy(s - 1, way, r).wait_recv()
-            ring_out[way, s, r] = ring_sums(s, way, r, sources[way])
-            ring_copy(s, way, r).start()
+        for late in range(2):
+            for way in range(2):
+                group = way if late else 1 - way
+                if late or s > 1:
+                    ring_copy(s - 1, way, group).wait_recv()
+                for r in LATE[group]:
+                    ring_out[way, s, SPOT[r]] = ring_sums(s, way, r, sources[way])
+                ring_copy(s, way, group).start()
 
     last = far_y - 1
     for s in range(1, last):
@@ -358,10 +358,13 @@
     part_copy(2 * last).wait_recv()
     part_copy(2 * last + 1).wait_recv()
     sources = [source_of(2 * last + way, 0) for way in range(2)]
-    for way, r in ORDER:
-        ring_copy(last - 1, way, r).wait_recv()
-        ring_out[way, last, r] = ring_sums(last, way, r, sources[way])
-        last_copy(way, r).start()
+    for late in range(2):
+        for way in range(2):
+            group = way if late else 1 - way
+            ring_copy(last - 1, way, group).wait_recv()
+            for r in LATE[group]:
+                ring_out[way, last, SPOT[r]] = ring_sums(last, way, r, sources[way])
+                last_copy(way, r).start()
 
     def left(ref, sem):
         copy(ref, ref, sem, f_recv.at[0], partner).wait_send()
@@ -433,7 +436,7 @@
             dma((2, 2)), dma((2, far, V)),
             dma((1,)), dma((X,)),
             dma((1,)), dma((Y,)),
-            dma((3,)), dma((2, far_y - 1, X)),
+            dma((3,)), dma((2, far_y - 1, 2)),
             dma((3,)), dma((3,)),
             dma((3 + Z,)),
         ],

time: 74.3 us -> 73.9 us (level)
  no operation moved by 1% of the time
where the time goes in v6:
time: 73.9 us; the launch traced here: 73.7 us
  Pallas kernels  72 us (97%)
  local copies, waits for them, and re-layouts  1.67 us (2%)
    pallas_call x1, Pallas kernels, per_device(): pl.pallas_call(functools.partial(kernel, Z, Y), out_shape=jax.ShapeDtypeS...  72 us
    unnamed x1, local copies, waits for them, and re-layouts  1.67 us

profile of v6, /device:TPU:1, one launch (start us, length us, event | category | flops | bytes accessed | tf_op | source)
XLA Modules:
  0.0 73.7 jit_solution(9464509220859405604)
XLA Ops:
  0.0 72.0 %shard_map.55 = bf16[2,4,128,128]{3,2,1,0:T(8,128)(2,1)} custom-call(bf16[2,8,128,128]{3,2,1,0:T(8,128)(2,1)} %amp_hbm.1, s32[2,8]{1,0:T(2,128)} %amp_mask.1, bf16[1,8,128,128]{3,2,1,0:T(8,128)(2,1)} %int_hbm.1, s32[1,8]{1,0:T(1,128)} %int_mask.1, s32[1,48]{1,0:T(1,128)} %bitcast.1), custom_call_target="tpu_custom_call" | custom-call | flops 2147483648 | bytes 1048576 | tf_op jit(solution)/shard_map/pallas_call | solution.py:412
  72.0 1.7 %copy.7 = bf16[2,4,128,128]{3,2,1,0:T(8,128)(2,1)} copy(bf16[2,4,128,128]{3,2,1,0:T(8,128)(2,1)} %shard_map.55) | data formatting | bytes 524288
